TPU v7x, 256 devices: a whole 4x4x8 slice. The times are simulated.
256 devices in a mesh: row: 32 (over x, y, core), col: 8 (over z).
Axes of the slice: x: 4, y: 4, z: 8, core: 2. Of those that a mesh axis runs over, the one named last changes fastest.
Arguments:
- activations: bfloat16 [32768, 16384], P('row', 'col'), may hold values from -200 to 200
- sketch: bfloat16 [16384, 512], P('col'), may hold values from -0.046875 to 0.046875
Outputs:
- scaled_basis: float32 [32768, 512], P('row')
- coefficients: float32 [512, 16384], P('row', 'col')
All inputs are finite; a program needn't handle non-finite values.
Results may differ from a plain program's by a relative error of at most 0.0047.
Values may be sent and summed in bfloat16 or wider, within the bound.
No kernel may reach another device: no remote copies, remote signals or barrier semaphores. Data moves between devices by JAX's collectives and lax.ppermute only.
A program may use at most 64 MiB of HBM per device.

v0:
```python
import math

import jax
import jax.numpy as jnp
from jax import lax
from jax.sharding import PartitionSpec as P


def sample_rows(activations, factor):
    share = lax.psum_scatter(
        jnp.dot(activations, factor, preferred_element_type=jnp.float32),
        "col",
        scatter_dimension=0,
        tiled=True,
    )
    return lax.all_gather(share, "col", axis=0, tiled=True)


def orthonormal(sampled):
    gram_matrix = jnp.dot(
        sampled.T, sampled, precision=lax.Precision.HIGHEST, preferred_element_type=jnp.float32
    )
    gram_matrix = lax.psum(gram_matrix, "row")
    lower_factor = jnp.linalg.cholesky(gram_matrix)
    return jax.scipy.linalg.solve_triangular(lower_factor, sampled.T, lower=True).T


def body(activations, sketch):
    rows_dev, cols_dev = activations.shape
    row_count = lax.axis_size("row")
    contract_rows = (((0,), (0,)), ((), ()))
    sampled = sample_rows(activations, sketch)
    basis_half = orthonormal(sampled).astype(jnp.bfloat16)
    partial_sum = lax.dot_general(
        activations, basis_half, contract_rows, preferred_element_type=jnp.float32
    )
    gathered = lax.psum(partial_sum, "row").astype(jnp.bfloat16)
    sampled = sample_rows(activations, gathered)
    basis_two = orthonormal(sampled)
    basis_half = basis_two.astype(jnp.bfloat16)
    coefficients = lax.psum_scatter(
        lax.dot_general(basis_half, activations, contract_rows, preferred_element_type=jnp.float32),
        "row",
        scatter_dimension=0,
        tiled=True,
    )
    scaled_basis = math.sqrt(rows_dev * row_count) * basis_two
    return (scaled_basis, coefficients)


def solution(mesh):
    in_specs = (P("row", "col"), P("col", None))
    out_specs = (P("row", None), P("row", "col"))
    return jax.shard_map(body, mesh=mesh, in_specs=in_specs, out_specs=out_specs, check_vma=False)
```

profile of v0, /device:TPU:2, one launch (start us, length us, event | category | flops | bytes accessed | tf_op | source)
XLA Modules:
  0.0 1004.6 jit_solution(10253179892958751541)
XLA Ops:
  8.8 5.8 fusion.88
  14.7 45.0 %reduce-scatter.4.cloned.1.call-done = f32[128,512]{1,0:T(8,128)} async-done(((f32[1024,512]{1,0:T(8,128)}), f32[128,512]{1,0:T(8,128)}) %reduce-scatter.4.cloned.1.call-update) | async-done | bytes 262160 | tf_op jit(solution)/shard_map/reduce_scatter | solution.py:10
  59.8 41.9 %all-gather.3.cloned.1.call-done = f32[1024,512]{1,0:T(8,128)} async-done(((f32[128,512]{1,0:T(8,128)}), f32[1024,512]{1,0:T(8,128)}) %all-gather.3.cloned.1.call-update) | async-done | bytes 2097168 | tf_op jit(solution)/shard_map/all_gather | solution.py:16
  101.7 6.7 fusion.89
  108.6 112.8 %all-reduce.5.cloned.1.call-done = f32[512,512]{0,1:T(8,128)} async-done(((f32[512,512]{0,1:T(8,128)}), f32[512,512]{0,1:T(8,128)}) %all-reduce.5.cloned.1.call-update) | async-done | bytes 1048592 | tf_op jit(solution)/shard_map/psum | solution.py:23
  226.5 11.7 %cholesky.286 = f32[128,128]{1,0:T(8,128)S(1)} custom-call(f32[128,128]{1,0:T(8,128)S(1)} %cholesky.426), custom_call_target="Cholesky" | custom-call | tf_op jit(solution)/shard_map/jit(cholesky)/cholesky | solution.py:24
  238.2 9.8 custom-call.27
  250.7 11.7 %cholesky.305 = f32[128,128]{1,0:T(8,128)S(1)} custom-call(f32[128,128]{1,0:T(8,128)S(1)} %cholesky.430), custom_call_target="Cholesky" | custom-call | tf_op jit(solution)/shard_map/jit(cholesky)/cholesky | solution.py:24
  262.4 10.2 %custom-call.28 = f32[1,128,128]{1,2,0:T(8,128)S(1)} custom-call(f32[1,128,128]{2,1,0:T(8,128)S(1)} %get-tuple-element.58), custom_call_target="InvertDiagBlocksLowerTriangular" | custom-call | tf_op jit(solution)/shard_map/jit(cholesky)/cholesky | solution.py:24
  274.2 11.7 %cholesky.326 = f32[128,128]{1,0:T(8,128)S(1)} custom-call(f32[128,128]{1,0:T(8,128)S(1)} %cholesky.435), custom_call_target="Cholesky" | custom-call | tf_op jit(solution)/shard_map/jit(cholesky)/cholesky | solution.py:24
  286.6 9.8 custom-call.29
  297.9 11.7 %cholesky.343 = f32[128,128]{1,0:T(8,128)S(1)} custom-call(f32[128,128]{1,0:T(8,128)S(1)} %convolution_subtract_fusion.9), custom_call_target="Cholesky" | custom-call | tf_op jit(solution)/shard_map/jit(cholesky)/cholesky | solution.py:24
  314.7 11.4 %while.4 = (s32[]{:T(128)}, f32[512,512]{1,0:T(8,128)}, s32[4,2]{0,1:T(2,128)S(1)}, f32[4,128,128]{2,1,0:T(8,128)S(1)}, s32[]{:T(128)}) while((s32[]{:T(128)}, f32[512,512]{1,0:T(8,128)}, s32[4,2]{0,1:T(2,128)S(1)}, f32[4,128,128]{2,1,0:T(8,128)S(1)}, s32[]{:T(128)}) %tuple.56), condition=%wide.while_cond, body=%wide.while_body.sunk | while | flops 2 | bytes 131181 | solution.py:25
  326.1 39.3 %custom-call.30 = f32[4,128,128]{1,2,0:T(8,128)S(1)} custom-call(f32[4,128,128]{2,1,0:T(8,128)S(1)} %get-tuple-element.18), custom_call_target="InvertDiagBlocksLowerTriangular" | custom-call | tf_op jit(solution)/shard_map/jit(_solve_triangular)/triangular_solve | solution.py:25
  378.1 4.3 convolution_bitcast_fusion
  382.4 132.8 %all-reduce.8 = bf16[2048,512]{0,1:T(8,128)(2,1)} all-reduce(f32[2048,512]{0,1:T(8,128)} %convolution_bitcast_fusion), channel_id=1, replica_groups=mesh['row'=32,'col'=8] {'row'}, use_global_device_ids=true, to_apply=%region_10.13 | all-reduce | flops 1048576 | bytes 6291456 | tf_op jit(solution)/shard_map/psum | solution.py:37
  515.2 6.5 fusion.2
  521.8 58.4 %reduce-scatter.6.cloned.1.call-done = f32[128,512]{0,1:T(8,128)} async-done(((f32[1024,512]{0,1:T(8,128)}), f32[128,512]{0,1:T(8,128)}) %reduce-scatter.6.cloned.1.call-update) | async-done | bytes 262160 | tf_op jit(solution)/shard_map/reduce_scatter | solution.py:10
  580.3 47.8 %all-gather.5.cloned.1.call-done = f32[1024,512]{0,1:T(8,128)} async-done(((f32[128,512]{0,1:T(8,128)}), f32[1024,512]{0,1:T(8,128)}) %all-gather.5.cloned.1.call-update) | async-done | bytes 2097168 | tf_op jit(solution)/shard_map/all_gather | solution.py:16
  628.1 6.7 fusion.90
  635.3 113.3 %all-reduce.7.cloned.1.call-done = f32[512,512]{0,1:T(8,128)} async-done(((f32[512,512]{0,1:T(8,128)}), f32[512,512]{0,1:T(8,128)}) %all-reduce.7.cloned.1.call-update) | async-done | bytes 1048592 | tf_op jit(solution)/shard_map/psum | solution.py:23
  753.7 11.7 %cholesky.358 = f32[128,128]{1,0:T(8,128)S(1)} custom-call(f32[128,128]{1,0:T(8,128)S(1)} %cholesky.439), custom_call_target="Cholesky" | custom-call | tf_op jit(solution)/shard_map/jit(cholesky)/cholesky | solution.py:24
  765.5 9.8 custom-call.31
  777.9 11.7 %cholesky.377 = f32[128,128]{1,0:T(8,128)S(1)} custom-call(f32[128,128]{1,0:T(8,128)S(1)} %cholesky.443), custom_call_target="Cholesky" | custom-call | tf_op jit(solution)/shard_map/jit(cholesky)/cholesky | solution.py:24
  790.9 9.9 custom-call.32
  802.5 11.7 %cholesky.398 = f32[128,128]{1,0:T(8,128)S(1)} custom-call(f32[128,128]{1,0:T(8,128)S(1)} %cholesky.448), custom_call_target="Cholesky" | custom-call | tf_op jit(solution)/shard_map/jit(cholesky)/cholesky | solution.py:24
  814.8 9.8 custom-call.33
  826.1 11.7 %cholesky.415 = f32[128,128]{1,0:T(8,128)S(1)} custom-call(f32[128,128]{1,0:T(8,128)S(1)} %convolution_subtract_fusion.8), custom_call_target="Cholesky" | custom-call | tf_op jit(solution)/shard_map/jit(cholesky)/cholesky | solution.py:24
  842.3 11.4 %while.5 = (s32[]{:T(128)}, f32[512,512]{1,0:T(8,128)}, s32[4,2]{0,1:T(2,128)S(1)}, f32[4,128,128]{2,1,0:T(8,128)S(1)}, s32[]{:T(128)}) while((s32[]{:T(128)}, f32[512,512]{1,0:T(8,128)}, s32[4,2]{0,1:T(2,128)S(1)}, f32[4,128,128]{2,1,0:T(8,128)S(1)}, s32[]{:T(128)}) %tuple.76), condition=%wide.while_cond.clone, body=%wide.while_body.clone.sunk | while | flops 2 | bytes 131181 | solution.py:25
  853.7 39.3 %custom-call.34 = f32[4,128,128]{1,2,0:T(8,128)S(1)} custom-call(f32[4,128,128]{2,1,0:T(8,128)S(1)} %get-tuple-element.19), custom_call_target="InvertDiagBlocksLowerTriangular" | custom-call | tf_op jit(solution)/shard_map/jit(_solve_triangular)/triangular_solve | solution.py:25
  903.5 4.3 fusion.24
  913.6 84.0 %reduce-scatter.8.cloned.1.call-done = f32[16,2048]{1,0:T(8,128)} async-done(((f32[512,2048]{1,0:T(8,128)}), f32[16,2048]{1,0:T(8,128)}) %reduce-scatter.8.cloned.1.call-update) | async-done | bytes 131088 | tf_op jit(solution)/shard_map/reduce_scatter | solution.py:41
  (121 shorter events, 82.6 us)
Async XLA Ops:
  7.2 1.6 copy-start
  7.2 52.5 %reduce-scatter.4.cloned.1.call-start = ((), (), s32[]{:S(2)}) async-start(), calls=%async_computation.3 | async-start | bytes 2359296 | tf_op jit(solution)/shard_map/reduce_scatter | solution.py:10
  14.6 87.0 %all-gather.3.cloned.1.call-start = ((), (), s32[]{:S(2)}) async-start(), calls=%async_computation.4 | async-start | bytes 2359296 | tf_op jit(solution)/shard_map/all_gather | solution.py:16
  59.7 161.7 %all-reduce.5.cloned.1.call-start = ((), (), s32[]{:S(2)}) async-start(), calls=%async_computation.5 | async-start | bytes 2097152 | tf_op jit(solution)/shard_map/psum | solution.py:23
  108.4 471.9 %reduce-scatter.6.cloned.1.call-start = ((), (), s32[]{:S(2)}) async-start(), calls=%async_computation.6 | async-start | bytes 2359296 | tf_op jit(solution)/shard_map/reduce_scatter | solution.py:10
  221.4 2.6 copy-start.4
  225.5 1.0 copy-start.7
  365.4 4.6 copy-start.1
  372.8 5.3 copy-start.9
  521.8 106.3 %all-gather.5.cloned.1.call-start = ((), (), s32[]{:S(2)}) async-start(), calls=%async_computation.7 | async-start | bytes 2359296 | tf_op jit(solution)/shard_map/all_gather | solution.py:16
  580.3 168.3 %all-reduce.7.cloned.1.call-start = ((), (), s32[]{:S(2)}) async-start(), calls=%async_computation.8 | async-start | bytes 2097152 | tf_op jit(solution)/shard_map/psum | solution.py:23
  634.8 362.8 %reduce-scatter.8.cloned.1.call-start = ((), (), s32[]{:S(2)}) async-start(), calls=%async_computation.9 | async-start | bytes 4325376 | tf_op jit(solution)/shard_map/reduce_scatter | solution.py:41
  748.6 2.6 copy-start.5
  752.7 1.0 copy-start.6
  893.0 4.1 copy-start.2
  898.8 4.7 copy-start.10
  899.5 3.2 copy-start.3
  902.7 0.8 copy-start.8
Sparse Core Ops, SparseCore 0:
  14.8 44.8 reduce-scatter.3
  61.5 40.1 all-gather.2
  108.5 112.8 all-reduce.4
  521.9 58.3 reduce-scatter.5
  581.9 46.0 all-gather.4
  634.9 113.6 all-reduce.6
  907.9 89.5 reduce-scatter.7
where the time goes:
time: 1010 us; the launch traced here: 1000 us
  waiting for transfers between devices  503 us (50%)
  other arithmetic  245 us (24%)
  blocking collectives  133 us (13%)
  matrix products  67.5 us (7%)
  local copies, waits for them, and re-layouts  35.4 us (4%)
  between operations  19.8 us (2%)
    psum x2, waiting for transfers between devices, orthonormal(): gram_matrix = lax.psum(gram_matrix, 'row')  226 us
    another operation x29, other arithmetic, orthonormal(): lower_factor = jnp.linalg.cholesky(gram_matrix)  158 us
    psum x1, blocking collectives, body(): gathered = lax.psum(partial_sum, 'row').astype(jnp.bfloat16)  133 us
    reduce_scatter x2, waiting for transfers between devices, sample_rows(): lax.psum_scatter(jnp.dot(activations, factor, preferred_element_type=jnp....  103 us
    all_gather x2, waiting for transfers between devices, sample_rows(): return lax.all_gather(share, 'col', axis=0, tiled=True)  89.7 us
    reduce_scatter x1, waiting for transfers between devices, body(): lax.psum_scatter(lax.dot_general(basis_half, activations, contract_rows,...  84 us
    another operation x5, other arithmetic, orthonormal(): jax.scipy.linalg.solve_triangular(lower_factor, sampled.T, lower=True)  81.2 us
    another operation x27, local copies, waits for them, and re-layouts, orthonormal(): jax.scipy.linalg.solve_triangular(lower_factor, sampled.T, lower=True)  22.7 us
  transfers between devices with their start and end apart: 7, of which 7 were waited for; matrix products, arithmetic and copies ran while one was open for 1% of the time, Pallas kernels for 0%

commit v1 on v0

v1 whole, which is shorter than its diff:
```python
import math

import jax
import jax.numpy as jnp
from jax import lax
from jax.experimental import pallas as pl
from jax.experimental.pallas import tpu as pltpu
from jax.sharding import PartitionSpec as P

F32 = jnp.float32
BF16 = jnp.bfloat16
HIGHEST = lax.Precision.HIGHEST
BLOCK = 128
PANEL = 8


def reciprocal(value):
    guess = pl.reciprocal(value, approx=True)
    guess = guess * (2.0 - value * guess)
    return guess * (2.0 - value * guess)


def factor_block(tiles):
    lane = lax.broadcasted_iota(jnp.int32, (PANEL, BLOCK), 1)
    sub = lax.broadcasted_iota(jnp.int32, (PANEL, BLOCK), 0)
    tiles = list(tiles)

    def over_lanes(tile, at):
        return jnp.broadcast_to(tile[:, at : at + 1], (PANEL, BLOCK))

    def over_rows(tile, at):
        return jnp.broadcast_to(tile[at : at + 1, :], (PANEL, BLOCK))

    for g in range(len(tiles)):
        first = PANEL * g
        pivot = [over_lanes(tiles[g], first + l) for l in range(PANEL)]
        entry = [[over_rows(pivot[l], m) for l in range(m + 1)] for m in range(PANEL)]
        ratio = [[None] * PANEL for _ in range(PANEL)]
        inverse = [None] * PANEL
        for j in range(PANEL):
            if j % 2 == 0:
                a, b, c = entry[j][j], entry[j + 1][j], entry[j + 1][j + 1]
                inverse[j] = reciprocal(a)
                inverse[j + 1] = a * reciprocal(a * c - b * b)
            for m in range(j + 1, PANEL):
                ratio[j][m] = entry[m][j] * inverse[j]
            for m in range(j + 1, PANEL):
                for l in range(j + 1, m + 1):
                    entry[m][l] = entry[m][l] - entry[m][j] * ratio[j][l]
        inside = (lane >= first) & (lane < first + PANEL)
        start = jnp.where(inside, jnp.where(lane == sub + first, 1.0, 0.0), tiles[g])
        rows = []
        for m in range(PANEL):
            row = over_rows(start, m)
            for l in range(m):
                row = row - ratio[l][m] * rows[l]
            rows.append(row)
        scaled = [rows[m] * inverse[m] for m in range(PANEL)]
        for i in range(g + 1, len(tiles)):
            columns = []
            total = jnp.where(inside, 0.0, tiles[i])
            for m in range(PANEL):
                column = over_lanes(tiles[i], first + m)
                for l in range(m):
                    column = column - ratio[l][m] * columns[l]
                columns.append(column)
                total = total - column * scaled[m]
            tiles[i] = total
        squared, own = inverse[0], rows[0]
        for m in range(1, PANEL):
            squared = jnp.where(sub == m, inverse[m], squared)
            own = jnp.where(sub == m, rows[m], own)
        tiles[g] = own * (squared * lax.rsqrt(squared))
    return tiles


def inverse_factor_kernel(gram_ref, out_ref, work):
    n = gram_ref.shape[0]
    row_at = lax.broadcasted_iota(jnp.int32, (n, n), 0)
    col_at = lax.broadcasted_iota(jnp.int32, (n, n), 1)
    gram = gram_ref[...]
    diagonal = jnp.where(row_at == col_at, gram, 0.0)
    scale_cols = lax.rsqrt(jnp.sum(diagonal, axis=0, keepdims=True))
    scale_rows = lax.rsqrt(jnp.sum(diagonal, axis=1, keepdims=True))
    work[...] = gram * (scale_rows * scale_cols)

    def step(k, carry):
        first = pl.multiple_of(k * BLOCK, BLOCK)
        own = pl.ds(first, BLOCK)
        block = work[own, own]
        tiles = factor_block([block[PANEL * i : PANEL * (i + 1), :] for i in range(BLOCK // PANEL)])
        ri = lax.broadcasted_iota(jnp.int32, (BLOCK, BLOCK), 0)
        ci = lax.broadcasted_iota(jnp.int32, (BLOCK, BLOCK), 1)
        lower_inverse = jnp.where(ci <= ri, jnp.concatenate(tiles, axis=0), 0.0)
        work[own, own] = jnp.where(ci == ri, 1.0, 0.0)
        rows = jnp.dot(lower_inverse, work[own, :], precision=HIGHEST, preferred_element_type=F32)
        cols = lax.broadcasted_iota(jnp.int32, (BLOCK, n), 1)
        upper = jnp.where(cols >= first + BLOCK, rows, 0.0)
        below = lax.broadcasted_iota(jnp.int32, (n, BLOCK), 0) >= first + BLOCK
        work[:, own] = jnp.where(below, 0.0, work[:, own])
        work[...] -= lax.dot_general(
            upper, rows, (((0,), (0,)), ((), ())), precision=HIGHEST, preferred_element_type=F32
        )
        work[own, :] = rows
        return carry

    lax.fori_loop(0, n // BLOCK, step, 0)
    out_ref[...] = jnp.where(col_at <= row_at, work[...], 0.0) * scale_cols


def inverse_factor(gram):
    n = gram.shape[0]
    return pl.pallas_call(
        inverse_factor_kernel,
        out_shape=jax.ShapeDtypeStruct((n, n), F32),
        scratch_shapes=[pltpu.VMEM((n, n), F32)],
        compiler_params=pltpu.CompilerParams(vmem_limit_bytes=16 << 20),
        cost_estimate=pl.CostEstimate(flops=2 * n**3, bytes_accessed=8 * n * n, transcendentals=4 * n),
    )(gram)


def exchange(pieces, axis, groups=None):
    return lax.all_to_all(pieces, axis, 0, 0, tiled=True, axis_index_groups=groups)


def spread(share, axis, count, groups=None):
    copies = lax.optimization_barrier(jnp.broadcast_to(share[None], (count,) + share.shape))
    return exchange(copies, axis, groups)


def swap_cores(array):
    rows = lax.axis_size("row")
    return lax.ppermute(array, "row", [(i, i ^ 1) for i in range(rows)])


def same_core():
    rows = lax.axis_size("row")
    return [list(range(core, rows, 2)) for core in range(2)]


def sum_gram(share):
    rows, cols = lax.axis_size("row"), lax.axis_size("col")
    part = lax.dot_general(
        share, share, (((0,), (0,)), ((), ())), precision=HIGHEST, preferred_element_type=F32
    )
    n = part.shape[0]
    own = jnp.sum(exchange(part.reshape(rows, n // rows, n), "row"), axis=0)
    own = jnp.sum(spread(own, "col", cols), axis=0)
    return spread(own, "row", rows).reshape(n, n)


def sum_rows(partial):
    core = lax.rem(lax.axis_index("row"), 2)
    away = lax.dynamic_index_in_dim(partial, 1 - core, 1, keepdims=False).astype(BF16)
    stay = lax.dynamic_index_in_dim(partial, core, 1, keepdims=False)
    pair = (stay + swap_cores(away).astype(F32)).astype(BF16)
    return jnp.sum(exchange(pair, "row", same_core()).astype(F32), axis=0)


def gather_rows(share):
    chips = lax.axis_size("row") // 2
    core = lax.rem(lax.axis_index("row"), 2)
    mine = spread(share, "row", chips, same_core())
    other = swap_cores(mine)
    first = jnp.where(core == 0, mine, other)
    second = jnp.where(core == 0, other, mine)
    return jnp.stack([first, second], axis=1)


def orthonormal(partial):
    share = lax.psum_scatter(partial, "col", scatter_dimension=0, tiled=True)
    sampled = lax.all_gather(share, "col", axis=0, tiled=True)
    lower_inverse = inverse_factor(sum_gram(share))
    return lax.dot_general(
        sampled, lower_inverse, (((1,), (1,)), ((), ())), precision=HIGHEST, preferred_element_type=F32
    )


def body(activations, sketch):
    rows_dev, cols_dev = activations.shape
    rank = sketch.shape[1]
    row_count = lax.axis_size("row")
    chips = row_count // 2
    contract_rows = (((0,), (0,)), ((), ()))
    basis_half = orthonormal(jnp.dot(activations, sketch, preferred_element_type=F32)).astype(BF16)
    partial_sum = lax.dot_general(activations, basis_half, contract_rows, preferred_element_type=F32)
    own = sum_rows(partial_sum.reshape(chips, 2, cols_dev // row_count, rank)).astype(BF16)
    gathered = gather_rows(own).reshape(cols_dev, rank)
    basis_two = orthonormal(jnp.dot(activations, gathered, preferred_element_type=F32))
    basis_half = basis_two.astype(BF16)
    projected = lax.dot_general(basis_half, activations, contract_rows, preferred_element_type=F32)
    coefficients = sum_rows(projected.reshape(chips, 2, rank // row_count, cols_dev))
    scaled_basis = math.sqrt(rows_dev * row_count) * basis_two
    return (scaled_basis, coefficients)


def solution(mesh):
    in_specs = (P("row", "col"), P("col", None))
    out_specs = (P("row", None), P("row", "col"))
    return jax.shard_map(body, mesh=mesh, in_specs=in_specs, out_specs=out_specs, check_vma=False)
```

time: 1010 us -> 398 us (0.39)
  waiting for transfers between devices: 503 us -> 104 us
  other arithmetic: 245 us -> 4.92 us
  Pallas kernels: 0 us -> 48 us
  matrix products: 67.5 us -> 35.5 us
  blocking collectives: 133 us -> 163 us
  local copies, waits for them, and re-layouts: 35.4 us -> 14.1 us
    another operation x34 -> x2, other arithmetic: 239 us -> 1.56 us  [gather_rows(): return jnp.stack([first, second], axis=1)]
    psum x2 -> x0, waiting for transfers between devices: 226 us -> none  [orthonormal(): gram_matrix = lax.psum(gram_matrix, 'row')]
    all_to_all x0 -> x8, blocking collectives: none -> 163 us  [exchange(): lax.all_to_all(pieces, axis, 0, 0, tiled=True, axis_index_groups=groups)]
    psum x1 -> x0, blocking collectives: 133 us -> none  [body(): gathered = lax.psum(partial_sum, 'row').astype(jnp.bfloat16)]
    reduce_scatter x3 -> x2, waiting for transfers between devices: 187 us -> 82.2 us  [orthonormal(): share = lax.psum_scatter(partial, 'col', scatter_dimension=0, tiled=True)]
    all_gather x2, waiting for transfers between devices: 89.7 us -> 0.02 us  [orthonormal(): sampled = lax.all_gather(share, 'col', axis=0, tiled=True)]
    pallas_call x0 -> x2, Pallas kernels: none -> 48 us  [inverse_factor(): pl.pallas_call(inverse_factor_kernel, out_shape=jax.ShapeDtypeStruct((n,...]
    another operation x26 -> x0, matrix products: 33.1 us -> none  [the longest x14 22.2 us: orthonormal(): jax.scipy.linalg.solve_triangular(lower_factor, sampled.T, lower=True)]
  transfers between devices with their start and end apart: 7 -> 8, of which waited for: 7 -> 6; matrix products, arithmetic and copies ran while one was open for 1% -> 1% of each run, Pallas kernels for 0% -> 12%
where the time goes in v1:
time: 398 us; the launch traced here: 392 us
  blocking collectives  163 us (41%)
  waiting for transfers between devices  104 us (26%)
  Pallas kernels  48 us (12%)
  matrix products  35.5 us (9%)
  between operations  14.4 us (4%)
  local copies, waits for them, and re-layouts  14.1 us (4%)
  starting transfers between devices  8.01 us (2%)
  other arithmetic  4.92 us (1%)
    all_to_all x8, blocking collectives, exchange(): lax.all_to_all(pieces, axis, 0, 0, tiled=True, axis_index_groups=groups)  163 us
    reduce_scatter x2, waiting for transfers between devices, orthonormal(): share = lax.psum_scatter(partial, 'col', scatter_dimension=0, tiled=True)  82.2 us
    pallas_call x2, Pallas kernels, inverse_factor(): pl.pallas_call(inverse_factor_kernel, out_shape=jax.ShapeDtypeStruct((n,...  48 us
    dot_general x2, matrix products, orthonormal(): lax.dot_general(sampled, lower_inverse, (((1,), (1,)), ((), ())), precisi...  15.2 us
    all_to_all x1, waiting for transfers between devices, exchange(): lax.all_to_all(pieces, axis, 0, 0, tiled=True, axis_index_groups=groups)  14.2 us
  transfers between devices with their start and end apart: 8, of which 6 were waited for; matrix products, arithmetic and copies ran while one was open for 1% of the time, Pallas kernels for 12%

profile of v1, /device:TPU:2, one launch (start us, length us, event | category | flops | bytes accessed | tf_op | source)
XLA Modules:
  0.0 392.4 jit_solution(6928003782811252976)
XLA Ops:
  7.2 1.5 copy-done
  8.8 5.8 %fusion.6 = f32[1024,512]{1,0:T(8,128)} fusion(bf16[1024,2048]{1,0:T(8,128)(2,1)} %param.2, bf16[2048,512]{1,0:T(8,128)(2,1)S(1)} %copy-done), kind=kOutput, calls=%fused_computation.18 | convolution fusion | flops 2147483648 | bytes 8388608 | tf_op jit(solution)/shard_map/dot_general | solution.py:185
  14.7 45.0 %reduce-scatter.3.cloned.1.call-done = f32[128,512]{1,0:T(8,128)} async-done(((f32[1024,512]{1,0:T(8,128)}), f32[128,512]{1,0:T(8,128)}) %reduce-scatter.3.cloned.1.call-update) | async-done | bytes 262160 | tf_op jit(solution)/shard_map/reduce_scatter | solution.py:171
  59.7 2.1 fusion.7
  61.7 21.6 %all_to_all.45 = f32[32,16,512]{2,1,0:T(8,128)S(1)} all-to-all(f32[32,16,512]{2,1,0:T(8,128)S(1)} %bitcast.51), channel_id=1, replica_groups=mesh['row'=32,'col'=8] {'row'}, dimensions={0} | all-to-all | bytes 2097152 | tf_op jit(solution)/shard_map/all_to_all | solution.py:123
  83.5 20.4 %all_to_all.46 = f32[8,16,512]{2,1,0:T(8,128)S(1)} all-to-all(f32[8,16,512]{2,1,0:T(8,128)S(1)} %broadcast_in_dim.10), channel_id=1, replica_groups=mesh['row'=32,'col'=8] {'col'}, dimensions={0} | all-to-all | bytes 524288 | tf_op jit(solution)/shard_map/all_to_all | solution.py:123
  103.9 1.1 broadcast_in_dim.11
  105.0 5.6 %all-to-all-start.2 = ((f32[32,16,512]{2,1,0:T(8,128)}), f32[32,16,512]{2,1,0:T(8,128)S(1)}, u32[]{:S(2)}, u32[]{:S(2)}) async-start(f32[32,16,512]{2,1,0:T(8,128)} %broadcast_in_dim.11), calls=%async_computation.3 | async-start | bytes 2097152 | tf_op jit(solution)/shard_map/all_to_all | solution.py:123
  110.8 14.2 %all-to-all-done.2 = f32[32,16,512]{2,1,0:T(8,128)S(1)} async-done(((f32[32,16,512]{2,1,0:T(8,128)}), f32[32,16,512]{2,1,0:T(8,128)S(1)}, u32[]{:S(2)}, u32[]{:S(2)}) %all-to-all-start.2) | async-done | bytes 1048608 | tf_op jit(solution)/shard_map/all_to_all | solution.py:123
  125.1 23.9 %shard_map.41 = f32[512,512]{1,0:T(8,128)S(1)} custom-call(f32[512,512]{1,0:T(8,128)S(1)} %bitcast.45), custom_call_target="tpu_custom_call" | custom-call | flops 268435456 | bytes 2097152 | tf_op jit(solution)/shard_map/pallas_call | solution.py:113
  149.9 5.5 %convolution_convert_fusion = bf16[1024,512]{1,0:T(8,128)(2,1)S(1)} fusion(f32[1024,512]{1,0:T(8,128)} %all-gather.3.cloned.1.call-done, f32[512,512]{1,0:T(8,128)} %copy-done.1), kind=kOutput, calls=%fused_computation.10 | convolution fusion | flops 3221749760 | bytes 4194304 | tf_op jit(solution)/shard_map/dot_general | solution.py:174
  155.4 4.4 %convolution_bitcast_fusion = f32[2048,512]{0,1:T(8,128)} fusion(bf16[1024,512]{1,0:T(8,128)(2,1)S(1)} %convolution_convert_fusion, bf16[1024,2048]{1,0:T(8,128)(2,1)S(1)} %copy-done.2), kind=kOutput, calls=%fused_computation | convolution fusion | flops 2147483648 | bytes 9437184 | tf_op jit(solution)/shard_map/dot_general | solution.py:186
  159.8 5.4 %copy.6 = f32[2048,512]{1,0:T(8,128)} copy(f32[2048,512]{0,1:T(8,128)} %convolution_bitcast_fusion) | data formatting | bytes 8388608 | tf_op jit(solution)/shard_map/dot_general | solution.py:186
  165.1 2.7 fusion.2
  168.9 2.5 collective-permute-done
  171.4 2.0 fusion.1
  173.4 20.7 %all_to_all.47 = bf16[16,64,512]{2,1,0:T(8,128)(2,1)S(1)} all-to-all(bf16[16,64,512]{2,1,0:T(8,128)(2,1)S(1)} %fusion.1), channel_id=1, replica_groups={{0,16,32,48,64,80,96,112,128,144,160,176,192,208,224,240},{8,24,40,56,7..., dimensions={0} | all-to-all | bytes 2097152 | tf_op jit(solution)/shard_map/all_to_all | solution.py:123
  194.3 19.6 %all_to_all.48 = bf16[16,64,512]{2,1,0:T(8,128)(2,1)S(1)} all-to-all(bf16[16,64,512]{2,1,0:T(8,128)(2,1)S(1)} %broadcast_in_dim.12), channel_id=1, replica_groups={{0,16,32,48,64,80,96,112,128,144,160,176,192,208,224,240},{8,24,40,56,7..., dimensions={0} | all-to-all | bytes 2097152 | tf_op jit(solution)/shard_map/all_to_all | solution.py:123
  213.9 2.8 collective-permute-done.1
  216.7 1.4 select_bitcast_fusion.1
  218.3 2.0 copy-done.3
  220.3 3.7 convolution_bitcast_fusion.1
  224.0 37.2 %reduce-scatter.5.cloned.1.call-done = f32[128,512]{0,1:T(8,128)} async-done(((f32[1024,512]{0,1:T(8,128)}), f32[128,512]{0,1:T(8,128)}) %reduce-scatter.5.cloned.1.call-update) | async-done | bytes 262160 | tf_op jit(solution)/shard_map/reduce_scatter | solution.py:171
  261.3 2.0 fusion.8
  263.3 21.4 %all_to_all.49 = f32[32,16,512]{2,1,0:T(8,128)S(1)} all-to-all(f32[32,16,512]{2,1,0:T(8,128)S(1)} %bitcast.52), channel_id=1, replica_groups=mesh['row'=32,'col'=8] {'row'}, dimensions={0} | all-to-all | bytes 2097152 | tf_op jit(solution)/shard_map/all_to_all | solution.py:123
  284.8 18.0 %all_to_all.50 = f32[8,16,512]{2,1,0:T(8,128)S(1)} all-to-all(f32[8,16,512]{2,1,0:T(8,128)S(1)} %broadcast_in_dim.13), channel_id=1, replica_groups=mesh['row'=32,'col'=8] {'col'}, dimensions={0} | all-to-all | bytes 524288 | tf_op jit(solution)/shard_map/all_to_all | solution.py:123
  303.0 20.9 %all_to_all.51 = f32[32,16,512]{2,1,0:T(8,128)S(1)} all-to-all(f32[32,16,512]{2,1,0:T(8,128)S(1)} %broadcast_in_dim.14), channel_id=1, replica_groups=mesh['row'=32,'col'=8] {'row'}, dimensions={0} | all-to-all | bytes 2097152 | tf_op jit(solution)/shard_map/all_to_all | solution.py:123
  323.9 24.1 %shard_map.42 = f32[512,512]{1,0:T(8,128)S(1)} custom-call(f32[512,512]{1,0:T(8,128)S(1)} %bitcast.46), custom_call_target="tpu_custom_call" | custom-call | flops 268435456 | bytes 2097152 | tf_op jit(solution)/shard_map/pallas_call | solution.py:113
  348.1 9.7 %broadcast_multiply_fusion = (f32[1024,512]{1,0:T(8,128)}, bf16[1024,512]{1,0:T(8,128)(2,1)S(1)}) fusion(f32[1024,512]{0,1:T(8,128)} %all-gather.5.cloned.1.call-done, f32[512,512]{1,0:T(8,128)S(1)} %shard_map.42), kind=kOutput, calls=%fused_computation.15 | convolution fusion | flops 3222274048 | bytes 6291456 | tf_op jit(solution)/shard_map/dot_general | solution.py:174
  357.9 2.4 fusion.4
  361.4 2.3 collective-permute-done.2
  364.0 20.7 %all_to_all.52 = bf16[16,16,2048]{2,1,0:T(8,128)(2,1)S(1)} all-to-all(bf16[16,16,2048]{2,1,0:T(8,128)(2,1)S(1)} %fusion), channel_id=1, replica_groups={{0,16,32,48,64,80,96,112,128,144,160,176,192,208,224,240},{8,24,40,56,7..., dimensions={0} | all-to-all | bytes 2097152 | tf_op jit(solution)/shard_map/all_to_all | solution.py:123
  (34 shorter events, 5.5 us)
Async XLA Ops:
  7.2 1.6 copy-start
  7.2 52.5 %reduce-scatter.3.cloned.1.call-start = ((), (), s32[]{:S(2)}) async-start(), calls=%async_computation.11 | async-start | bytes 2359296 | tf_op jit(solution)/shard_map/reduce_scatter | solution.py:171
  14.6 135.3 %all-gather.3.cloned.1.call-start = ((), (), s32[]{:S(2)}) async-start(), calls=%async_computation.12 | async-start | bytes 2359296 | tf_op jit(solution)/shard_map/all_gather | solution.py:172
  105.0 20.1 %all-to-all-start.2 = ((f32[32,16,512]{2,1,0:T(8,128)}), f32[32,16,512]{2,1,0:T(8,128)S(1)}, u32[]{:S(2)}, u32[]{:S(2)}) async-start(f32[32,16,512]{2,1,0:T(8,128)} %broadcast_in_dim.11), calls=%async_computation.3 | async-start | bytes 2097152 | tf_op jit(solution)/shard_map/all_to_all | solution.py:123
  110.6 150.6 %reduce-scatter.5.cloned.1.call-start = ((), (), s32[]{:S(2)}) async-start(), calls=%async_computation.13 | async-start | bytes 2359296 | tf_op jit(solution)/shard_map/reduce_scatter | solution.py:171
  149.0 1.0 copy-start.1
  149.9 5.5 %copy-start.2 = (bf16[1024,2048]{1,0:T(8,128)(2,1)S(1)}, bf16[1024,2048]{1,0:T(8,128)(2,1)}, u32[]{:S(2)}) copy-start(bf16[1024,2048]{1,0:T(8,128)(2,1)} %param.2) | copy-start | bytes 12582916
  167.8 3.6 collective-permute-start
  213.9 2.8 collective-permute-start.1
  218.1 2.2 copy-start.3
  224.0 124.1 %all-gather.5.cloned.1.call-start = ((), (), s32[]{:S(2)}) async-start(), calls=%async_computation.14 | async-start | bytes 2359296 | tf_op jit(solution)/shard_map/all_gather | solution.py:172
  348.1 9.7 %copy-start.4 = (bf16[1024,2048]{1,0:T(8,128)(2,1)S(1)}, bf16[1024,2048]{1,0:T(8,128)(2,1)}, u32[]{:S(2)}) copy-start(bf16[1024,2048]{1,0:T(8,128)(2,1)} %param.2) | copy-start | bytes 12582916
  360.4 3.3 collective-permute-start.2
Sparse Core Ops, SparseCore 0:
  14.7 44.8 reduce-scatter.2
  61.4 44.9 all-gather.2
  224.1 37.1 reduce-scatter.4
  262.8 52.2 all-gather.4
